TPU v7x, 32 devices: a whole 2x2x4 slice. The times are simulated.
32 devices in a mesh: grp: 2 (over x), sfc: 16 (over z, y, core).
Axes of the slice: x: 2, y: 2, z: 4, core: 2. Of those that a mesh axis runs over, the one named last changes fastest.
Arguments:
- charges: bfloat16 [512, 8, 256], P(('grp', 'sfc')), parts along dimension 0, may hold values from -6 to 6
- self_blocks: bfloat16 [512, 256, 256], P(('grp', 'sfc')), parts along dimension 0, may hold values from -0.375 to 0.375
- near_blocks: bfloat16 [1024, 256, 256], P(('grp', 'sfc')), parts along dimension 0, may hold values from -0.375 to 0.375
- near_pairs: int32 [1024, 2], P(('grp', 'sfc')), parts along dimension 0, may hold values from 0 to 255, as said below
- bases: bfloat16 [512, 64, 256], P(('grp', 'sfc')), parts along dimension 0, may hold values from -0.375 to 0.375
- transfers: bfloat16 [512, 64, 64], P(('grp', 'sfc')), parts along dimension 0, may hold values from -0.75 to 0.75
- parent_of: int32 [512], P(('grp', 'sfc')), parts along dimension 0, may hold values from 0 to 127, as said below
- far_pairs: int32 [4096, 2], P(('grp', 'sfc')), parts along dimension 0, may hold values from -1 to 255, as said below
- far_coupling: bfloat16 [4096, 64, 64], P(('grp', 'sfc')), parts along dimension 0, may hold values from -0.75 to 0.75
- par_pairs: int32 [1024, 2], P(('grp', 'sfc')), parts along dimension 0, may hold values from 0 to 127, as said below
- par_coupling: bfloat16 [1024, 64, 64], P(('grp', 'sfc')), parts along dimension 0, may hold values from -0.75 to 0.75
Outputs:
- potentials: float32 [512, 8, 256], P(('grp', 'sfc')), parts along dimension 0
There are 2 independent parts, one for each index of `grp`. A program takes and returns all parts, laid end to end along the dimension named above; each array names one. Nothing has to cross between parts.
Inputs may be any that keep to these rules, and one draw needn't show every extreme that they name: `near_pairs`: slot s lies on device d = s // 32; column 0 is a leaf of device d (leaves d * 16 to (d + 1) * 16 - 1), column 1 a different leaf of device d or of device d + 1; on the last device only of device d. `parent_of`: leaves of device d have parents of device d (parents d * 8 to (d + 1) * 8 - 1), non-decreasing along the leaves; every parent has at least one child. `far_pairs`: the 128 slots of device d form 16 buckets of 8 slots; column 0 is always a leaf of device d; in bucket k a live slot has column 1 a leaf of device k (different from column 0 when k = d), an empty slot has -1; live slots come first in a bucket. At most 8 live slots a bucket, and every device has a full bucket. `par_pairs`: pair s lies on device d = s // 32; column 0 is a parent of device d, column 1 any other parent.
All inputs are finite; a program needn't handle non-finite values.
Results may differ from a plain program's by a relative error of at most 0.004.
Values may be sent and summed in bfloat16 or wider, within the bound.
No kernel may reach another device: no remote copies, remote signals or barrier semaphores. Data moves between devices by JAX's collectives and lax.ppermute only.
A program may use at most 128 MiB of HBM per device.

v0:
```python
import functools

import jax
import jax.numpy as jnp
from jax import lax
from jax.experimental import pallas as pl
from jax.experimental.pallas import tpu as pltpu
from jax.sharding import PartitionSpec as P

F32 = jnp.float32
BF16 = jnp.bfloat16
LANES = 128


def dot_nn(a, b):
    return lax.dot_general(a, b, (((1,), (0,)), ((), ())), preferred_element_type=F32)


def dot_nt(a, b):
    return lax.dot_general(a, b, (((1,), (1,)), ((), ())), preferred_element_type=F32)


def dot_tn(a, b):
    return lax.dot_general(a, b, (((0,), (0,)), ((), ())), preferred_element_type=F32)


def split2(x):
    high = x.astype(BF16)
    return high, (x - high.astype(F32)).astype(BF16)


def iota(shape, axis):
    return lax.broadcasted_iota(jnp.int32, shape, axis)


def one_hot(condition):
    return jnp.where(condition, 1.0, 0.0).astype(BF16)


def rows_to_lanes(ref, count, rhs):
    return jnp.concatenate([ref[pl.ds(r, count, stride=rhs), :] for r in range(rhs)], axis=1)


def lanes_to_rows(ref, value, rhs):
    count, width = value.shape
    rank = width // rhs
    for r in range(rhs):
        ref[pl.ds(r, count, stride=rhs), :] = value[:, r * rank : (r + 1) * rank]


def repeated(values, times):
    count = values.shape[1]
    spread = one_hot(iota((count, count * times), 1) // times == iota((count, count * times), 0))
    rows = jnp.broadcast_to(values.astype(F32), (8, count)).astype(BF16)
    return dot_nn(rows, spread)[0:1].astype(jnp.int32)


def by_rows(targets, parents, rhs):
    shape = (parents * rhs, targets.shape[1] * rhs)
    row, column = iota(shape, 0), iota(shape, 1)
    same = (repeated(targets % parents, rhs) == row // rhs) & (row % rhs == column % rhs)
    return jnp.where(same, 1.0, 0.0)


def row_sums(parts):
    row = iota(parts[0].shape, 0)
    for step in (4, 2, 1):
        upper = row % (2 * step) >= step
        merged = []
        for a, b in zip(parts[:step], parts[step:]):
            swapped = jnp.where(upper, a, b)
            if step == 4:
                moved = pltpu.roll(swapped, 4, axis=0)
            else:
                moved = jnp.where(
                    upper,
                    pltpu.roll(swapped, step, axis=0),
                    pltpu.roll(swapped, 8 - step, axis=0),
                )
            merged.append(jnp.where(upper, b, a) + moved)
        parts = merged
    return parts[0]


def fetch(pairs, sems):
    copies = [pltpu.make_async_copy(src, dst, sems.at[i]) for i, (src, dst) in enumerate(pairs)]
    for copy in copies:
        copy.start()
    return copies


def pre_kernel(
    charges_h,
    bases_h,
    transfers_h,
    parent_of_h,
    far_pairs_h,
    far_c_h,
    par_pairs_h,
    par_c_h,
    send,
    token,
    charges,
    bases,
    transfers,
    parent_of,
    far_pairs,
    far_c,
    par_pairs,
    par_c,
    par_smem,
    sems,
    mo,
    ch,
    pm3,
    pb,
    a_ref,
    ob,
):
    token[...] = jnp.zeros_like(token)
    leaves, rhs, _ = charges.shape
    rank = bases.shape[1]
    width = rhs * rank
    slots = far_c.shape[2]
    pairs = par_c.shape[0]
    parents = leaves // 2
    rows = send.shape[0]
    copies = fetch(
        [
            (parent_of_h, parent_of),
            (far_pairs_h, far_pairs),
            (par_pairs_h, par_pairs),
            (charges_h, charges),
            (bases_h, bases),
            (transfers_h, transfers),
            (par_pairs_h, par_smem),
            (far_c_h, far_c),
            (par_c_h, par_c),
        ],
        sems,
    )
    for copy in copies[:3]:
        copy.wait()
    to_parent = by_rows(parent_of[...], parents, rhs).astype(BF16)
    owner_hot = one_hot(far_pairs[0:1, :] % leaves == iota((leaves, slots), 0))
    partner_hot = one_hot(par_pairs[1:2, :] == iota((rows, pairs), 0))
    partner = far_pairs[1:2, :]
    local = jnp.where(partner >= 0, partner % leaves, -1).astype(F32)
    ob[width : width + LANES, :] = jnp.broadcast_to(local, (LANES, slots)).astype(BF16)
    unit = one_hot(iota((LANES, LANES), 0) == iota((LANES, LANES), 1))

    for copy in copies[3:5]:
        copy.wait()
    ms = [dot_nt(charges[l], bases[l]).astype(BF16) for l in range(leaves)]
    for l in range(leaves):
        mo[l * rhs : (l + 1) * rhs, :] = ms[l].astype(F32)
    copies[5].wait()
    for l in range(leaves):
        ch[l * rhs : (l + 1) * rhs, :] = dot_nt(ms[l], transfers[l])
    m2 = rows_to_lanes(mo, leaves, rhs)
    a_ref[...] = dot_tn(m2.astype(BF16), owner_hot)
    high, low = split2(ch[...])
    pm3[...] = (dot_nn(to_parent, high) + dot_nn(to_parent, low)).astype(BF16).astype(F32)
    for copy in copies[6:]:
        copy.wait()
    pm = rows_to_lanes(pm3, parents, rhs)
    half = 3 * width // 2
    shared = [
        jnp.concatenate([x[:, c * width // 2 : (c + 1) * width // 2] for x in (m2[:parents], m2[parents:], pm)], axis=1)
        for c in range(2)
    ]
    shared = jnp.concatenate(shared, axis=0).astype(BF16)
    at = 2 * width + LANES
    for p in range(rows // (2 * parents)):
        send[p * 2 * parents : (p + 1) * 2 * parents, at : at + half] = shared

    def parent_products(first, last):
        for s in range(first, last):
            q = par_smem[0, s] % parents
            x = pm3[pl.ds(pl.multiple_of(q * rhs, rhs), rhs), :].astype(BF16)
            pb[s * rhs : (s + 1) * rhs, :] = dot_nn(x, par_c[s])

    some = rank // 4
    parent_products(0, pairs // 4)
    for sb in range(slots // LANES):
        lanes = slice(sb * LANES, (sb + 1) * LANES)
        for part in range(4):
            first = part * some
            acc = [None] * rhs
            for k in range(rank):
                c = far_c[k, first : first + some, lanes].astype(F32)
                for r in range(rhs):
                    term = c * a_ref[r * rank + k : r * rank + k + 1, lanes]
                    acc[r] = term if k == 0 else acc[r] + term
            for r in range(rhs):
                at = r * rank + first
                ob[at : at + some, lanes] = acc[r].astype(BF16)
            if sb == 0 and part < 2:
                parent_products(pairs // 4 * (part + 1), pairs // 4 * (part + 2))
            if sb == 0 and part == 2:
                parent_products(pairs // 4 * 3, pairs)
                high, low = split2(rows_to_lanes(pb, pairs, rhs))
                at = width + LANES
                sums = dot_nn(partner_hot, high) + dot_nn(partner_hot, low)
                send[:, at : at + width] = sums.astype(BF16)
    for sb in range(slots // LANES):
        lanes = slice(sb * LANES, (sb + 1) * LANES)
        send[lanes, 0 : width + LANES] = dot_nt(unit, ob[:, lanes]).astype(BF16)


def near_kernel(pairs, earlier, charges, self_blocks, near_blocks, own, away, out):
    leaves = charges.shape[0]
    step = pl.program_id(0)
    selves, nears = self_blocks.shape[0], near_blocks.shape[0]

    @pl.when(step == 0)
    def _():
        out[...] = jnp.zeros_like(out)

    terms = []
    for i in range(selves):
        l = step * selves + i
        terms.append((l, dot_nt(charges[l], self_blocks[i])))
    for i in range(nears):
        a, b = pairs[0, step * nears + i], pairs[1, step * nears + i]
        first = (a // leaves) * leaves
        a, b = a - first, b - first
        x = charges[b % leaves]
        x = jnp.where(b < leaves, x, jnp.zeros_like(x))
        terms.append((a, dot_nt(x, near_blocks[i])))
        terms.append((b, dot_nn(charges[a], near_blocks[i])))
    for at, term in terms:
        out[at] += term

    @pl.when(step == pl.num_programs(0) - 1)
    def _():
        own[...] = out[0:leaves]
        away[...] = out[leaves:].astype(BF16)


def cross_kernel(pairs, near_own, following, near_blocks, total):
    leaves = following.shape[0]
    step = pl.program_id(0)
    nears = near_blocks.shape[0]

    @pl.when(step == 0)
    def _():
        total[...] = near_own[...]

    terms = []
    for i in range(nears):
        a, b = pairs[0, step * nears + i], pairs[1, step * nears + i]
        first = (a // leaves) * leaves
        a, b = a - first, b - first

        x = following[b % leaves]
        x = jnp.where(b >= leaves, x, jnp.zeros_like(x))
        terms.append((a, dot_nt(x, near_blocks[i])))
    for at, term in terms:
        total[at] += term


def far_gather(mom, far_pairs, b_ref, leaves, parents):
    rows, slots = mom.shape[0], b_ref.shape[1]
    wide = mom.shape[1] // 3
    row_id = iota((rows, slots), 0)
    base_leaf = row_id // parents * leaves + row_id % parents
    partner = far_pairs[1:2, :]
    total = None
    for h in range(2):
        hot = one_hot(partner == base_leaf + h * parents)
        part = dot_tn(mom[:, h * wide : (h + 1) * wide], hot)
        total = part if total is None else total + part
    b_ref[...] = total


def far_chunks(far_c, b_ref, fw):
    rank, slots = far_c.shape[0], far_c.shape[2]
    some = b_ref.shape[0] // rank

    def chunk(sb, k8):
        lanes = slice(sb * LANES, (sb + 1) * LANES)
        parts = [[] for _ in range(some)]
        for i in range(8):
            c = far_c[k8 * 8 + i, :, lanes].astype(F32)
            for r in range(some):
                prod = c * b_ref[r * rank : (r + 1) * rank, lanes]
                parts[r].append(sum(prod[j * 8 : (j + 1) * 8] for j in range(rank // 8)))
        for r in range(some):
            first = r * rank + k8 * 8
            fw[first : first + 8, lanes] = row_sums(parts[r])

    return [
        functools.partial(chunk, sb, k8) for sb in range(slots // LANES) for k8 in range(rank // 8)
    ]


def far_scatter(far_pairs, fw, leaves):
    hot = one_hot(far_pairs[0:1, :] % leaves == iota((leaves, fw.shape[1]), 0))
    high, low = split2(fw[...])
    return dot_nt(hot, high) + dot_nt(hot, low)


def far_kernel(
    got,
    far_pairs,
    far_c,
    par_pairs,
    parent_of,
    par_c,
    half,
    back,
    par_t,
    pick,
    to_owner,
    to_leaf,
    b_ref,
    fw,
):
    leaves, width = back.shape
    parents = leaves // 2
    rows = got.shape[0]
    index = got[:, width : width + LANES].astype(F32)[:, :leaves].astype(jnp.int32)
    hot = one_hot(index == iota((rows, leaves), 1))
    back[...] = dot_tn(hot, got[:, 0:width])
    mom = got[:, 2 * width + LANES :]
    far_gather(mom, far_pairs, b_ref, leaves, parents)
    for chunk in far_chunks(far_c, b_ref, fw):
        chunk()
    half[...] = far_scatter(far_pairs, fw, leaves)

    pairs = par_c.shape[0]
    rhs = to_owner.shape[0] // parents
    for s in range(pairs):
        par_t[s] = par_c[s].astype(F32).T.astype(BF16)
    hot = jnp.where(par_pairs[1:2, :] == iota((rows, pairs), 0), 1.0, 0.0)
    pick[...] = hot.T.astype(BF16)
    to_owner[...] = by_rows(par_pairs[0:1, :], parents, rhs).astype(BF16)
    to_leaf[...] = by_rows(parent_of[...], parents, rhs).T.astype(BF16)


def post_kernel(
    core_smem,
    half,
    back,
    mom2,
    got,
    bases,
    transfers,
    far_pairs,
    far_c,
    par_t,
    pick,
    to_owner,
    to_leaf,
    near_own,
    near_back,
    out,
    b_ref,
    fw,
    g_ref,
    pf,
    lf,
    pb,
    dn,
):
    leaves, rank, _ = bases.shape
    width = back.shape[1]
    rhs = width // rank
    pairs = par_t.shape[0]
    parents = leaves // 2
    rows = got.shape[0]
    core = core_smem[0, 0] // leaves % 2

    def in_order(mine, other):
        return jnp.concatenate(
            [jnp.where(core == 0, mine, other), jnp.where(core == 0, other, mine)], axis=1
        )

    wide = mom2.shape[1] // 3
    shared = in_order(got[:, got.shape[1] - wide :], mom2[:, 2 * wide :])
    fold = one_hot(iota((parents, rows), 1) % parents == iota((parents, rows), 0))
    at = width + LANES
    lanes_to_rows(pb, dot_nn(fold, got[:, at : at + width]), rhs)
    far_gather(mom2[...], far_pairs, b_ref, leaves, parents)
    chunks = far_chunks(far_c, b_ref, fw)
    each = len(chunks) // 8

    def some_chunks(group):
        for chunk in chunks[group * each : (group + 1) * each]:
            chunk()

    picked = dot_nn(pick[...], shared)
    some_chunks(0)
    lanes_to_rows(g_ref, picked, rhs)
    for s in range(pairs):
        at = slice(s * rhs, (s + 1) * rhs)
        pf[at, :] = dot_nn(g_ref[at, :].astype(BF16), par_t[s])
        if s % (pairs // 4) == pairs // 4 - 1:
            some_chunks(1 + s // (pairs // 4))
    high, low = split2(pf[...])
    locals_p = dot_nn(to_owner[...], high) + dot_nn(to_owner[...], low) + pb[...]
    some_chunks(5)
    picked = dot_nn(to_leaf[...], locals_p.astype(BF16))
    some_chunks(6)
    some_chunks(7)
    for l in range(leaves):
        at = slice(l * rhs, (l + 1) * rhs)
        dn[at, :] = dot_nn(picked[at, :].astype(BF16), transfers[l])

    other = far_scatter(far_pairs, fw, leaves)
    lanes_to_rows(lf, back[...] + in_order(half[...], other), rhs)
    for l in range(leaves):
        at = slice(l * rhs, (l + 1) * rhs)
        mine = (lf[at, :] + dn[at, :]).astype(BF16)
        near = near_own[l] + near_back[l].astype(F32)
        out[l] = dot_nn(mine, bases[l]) + near


def after(value, earlier, vmem_limit):
    anywhere = pl.BlockSpec(memory_space=pl.ANY)
    return pl.pallas_call(
        lambda *refs: None,
        out_shape=jax.ShapeDtypeStruct(value.shape, value.dtype),
        in_specs=[anywhere] * (1 + len(earlier)),
        out_specs=anywhere,
        input_output_aliases={0: 0},
        compiler_params=pltpu.CompilerParams(vmem_limit_bytes=vmem_limit),
        name="after",
    )(value, *earlier)


def passed_along(value, axis, steps):
    count = lax.axis_size(axis)
    leading, last = (max(0, -steps), min(count, count - steps))
    return lax.ppermute(value, axis, [(source, source + steps) for source in range(leading, last)])


def on_device(
    charges,
    self_blocks,
    near_blocks,
    near_pairs,
    bases,
    transfers,
    parent_of,
    far_pairs,
    far_coupling,
    par_pairs,
    par_coupling,
):
    leaves, rhs, panels = charges.shape
    rank = bases.shape[1]
    width = rhs * rank
    slots = far_coupling.shape[0]
    pairs = par_coupling.shape[0]
    parents = leaves // 2
    devices = lax.axis_size("sfc")
    rows = devices * parents
    columns = 2 * width + LANES + 3 * width // 2
    vmem = pl.BlockSpec(memory_space=pltpu.VMEM)
    smem = pl.BlockSpec(memory_space=pltpu.SMEM)
    hbm = pl.BlockSpec(memory_space=pltpu.HBM)
    params = pltpu.CompilerParams(vmem_limit_bytes=60 * 1024 * 1024)
    late = pltpu.CompilerParams(vmem_limit_bytes=48 * 1024 * 1024)

    def cost(moved):
        return pl.CostEstimate(flops=4 * moved, bytes_accessed=moved, transcendentals=0)

    following = passed_along(charges, "sfc", -1)
    far_pairs = far_pairs.T
    par_pairs = par_pairs.T
    near_pairs = near_pairs.T
    far_c = jnp.transpose(far_coupling, (1, 2, 0))
    parent_of = parent_of.reshape(1, leaves)

    def like(value, memory=pltpu.VMEM):
        return memory(value.shape, value.dtype)

    send, token = pl.pallas_call(
        pre_kernel,
        out_shape=[
            jax.ShapeDtypeStruct((rows, columns), BF16),
            jax.ShapeDtypeStruct((8, LANES), F32),
        ],
        in_specs=[hbm] * 8,
        out_specs=[vmem] * 2,
        scratch_shapes=[
            like(charges),
            like(bases),
            like(transfers),
            like(parent_of),
            like(far_pairs),
            like(far_c),
            like(par_pairs),
            like(par_coupling),
            like(par_pairs, pltpu.SMEM),
            pltpu.SemaphoreType.DMA((9,)),
            pltpu.VMEM((leaves * rhs, rank), F32),
            pltpu.VMEM((leaves * rhs, rank), F32),
            pltpu.VMEM((parents * rhs, rank), F32),
            pltpu.VMEM((pairs * rhs, rank), F32),
            pltpu.VMEM((width, slots), F32),
            pltpu.VMEM((width + LANES, slots), BF16),
        ],
        compiler_params=params,
        cost_estimate=cost(10_000_000),
        name="upward",
    )(charges, bases, transfers, parent_of, far_pairs, far_c, par_pairs, par_coupling)
    got = lax.all_to_all(send, "sfc", split_axis=0, concat_axis=0, tiled=True)
    steps = 4
    selves, nears = leaves // steps, near_blocks.shape[0] // steps
    whole = lambda *shape: pl.BlockSpec(shape, lambda i: (0,) * len(shape))
    near_params = pltpu.CompilerParams(vmem_limit_bytes=52 * 1024 * 1024)
    near_own, near_away = pl.pallas_call(
        near_kernel,
        grid=(steps,),
        out_shape=[
            jax.ShapeDtypeStruct((leaves, rhs, panels), F32),
            jax.ShapeDtypeStruct((leaves, rhs, panels), BF16),
        ],
        in_specs=[
            smem,
            pl.BlockSpec(memory_space=pl.ANY),
            whole(leaves, rhs, panels),
            pl.BlockSpec((selves, panels, panels), lambda i: (i, 0, 0)),
            pl.BlockSpec((nears, panels, panels), lambda i: (i, 0, 0)),
        ],
        out_specs=[whole(leaves, rhs, panels)] * 2,
        scratch_shapes=[pltpu.VMEM((2 * leaves, rhs, panels), F32)],
        compiler_params=near_params,
        cost_estimate=cost(20_000_000),
        name="near",
    )(near_pairs, token, charges, self_blocks, near_blocks)
    near_own = pl.pallas_call(
        cross_kernel,
        grid=(steps,),
        out_shape=jax.ShapeDtypeStruct((leaves, rhs, panels), F32),
        in_specs=[
            smem,
            whole(leaves, rhs, panels),
            whole(leaves, rhs, panels),
            pl.BlockSpec((nears, panels, panels), lambda i: (i, 0, 0)),
        ],
        out_specs=whole(leaves, rhs, panels),
        compiler_params=near_params,
        cost_estimate=cost(8_000_000),
        name="cross",
    )(near_pairs, near_own, following, near_blocks)
    near_back = passed_along(near_away, "sfc", 1)

    got = after(got, [near_back, near_own], 1 << 20)
    mom2 = lax.ppermute(
        got[:, 2 * width + LANES :], "sfc", [(i, i ^ 1) for i in range(devices)]
    )

    half, back, *prepared = pl.pallas_call(
        far_kernel,
        out_shape=[
            jax.ShapeDtypeStruct((leaves, width // 2), F32),
            jax.ShapeDtypeStruct((leaves, width), F32),
            jax.ShapeDtypeStruct(par_coupling.shape, BF16),
            jax.ShapeDtypeStruct((pairs, rows), BF16),
            jax.ShapeDtypeStruct((parents * rhs, pairs * rhs), BF16),
            jax.ShapeDtypeStruct((leaves * rhs, parents * rhs), BF16),
        ],
        in_specs=[vmem] * 6,
        out_specs=[vmem] * 6,
        scratch_shapes=[pltpu.VMEM((width // 2, slots), F32)] * 2,
        compiler_params=late,
        cost_estimate=cost(8_000_000),
        name="far",
    )(got, far_pairs, far_c, par_pairs, parent_of, par_coupling)

    return pl.pallas_call(
        post_kernel,
        out_shape=jax.ShapeDtypeStruct((leaves, rhs, panels), F32),
        in_specs=[smem] + [vmem] * 14,
        out_specs=vmem,
        scratch_shapes=[
            pltpu.VMEM((width // 2, slots), F32),
            pltpu.VMEM((width // 2, slots), F32),
            pltpu.VMEM((pairs * rhs, rank), F32),
            pltpu.VMEM((pairs * rhs, rank), F32),
            pltpu.VMEM((leaves * rhs, rank), F32),
            pltpu.VMEM((parents * rhs, rank), F32),
            pltpu.VMEM((leaves * rhs, rank), F32),
        ],
        compiler_params=late,
        name="downward",
    )(
        far_pairs,
        half,
        back,
        mom2,
        got,
        bases,
        transfers,
        far_pairs,
        far_c,
        *prepared,
        near_own,
        near_back,
    )


def solution(mesh):
    split = ("grp", "sfc")
    cube, flat = P(split, None, None), P(split, None)
    placed = (cube, cube, cube, flat, cube, cube, P(split), flat, cube, flat, cube)
    return jax.shard_map(
        on_device, mesh=mesh, in_specs=placed, out_specs=cube, check_vma=False
    )
```

profile of v0, /device:TPU:0, one launch (start us, length us, event | category | flops | bytes accessed | tf_op | source)
XLA Modules:
  0.0 33.2 jit_solution(3976752350636559667)
XLA Ops:
  0.0 4.3 %upward.1 = (bf16[128,1920]{1,0:T(8,128)(2,1)}, f32[8,128]{1,0:T(8,128)}) custom-call(bf16[16,8,256]{2,1,0:T(8,128)(2,1)} %charges.1, bf16[16,64,256]{2,1,0:T(8,128)(2,1)} %bases.1, bf16[16,64,64]{2,1,0:T(8,128)(2,1)} %transfers.1, s32[1,16]{1,0:T(1,128)} %bitcast.19, s32[2,128]{1,0:T(2,128)} %bitcast.11, bf16[64,64,128]{2,1,0:T(8,128)(2,1)} %bitcast.8, ...), custom_call_target="tpu_custom_call" | custom-call | flops 40000000 | bytes 10000000 | tf_op jit(solution)/shard_map/upward/pallas_call | solution.py:480
  4.3 7.4 %all-to-all-start = ((bf16[16,8,1920]{2,1,0:T(8,128)(2,1)}), bf16[16,8,1920]{2,1,0:T(8,128)(2,1)S(1)}, u32[]{:S(2)}, u32[]{:S(2)}) async-start(bf16[16,8,1920]{2,1,0:T(8,128)(2,1)} %bitcast.21), calls=%async_computation | async-start | bytes 983040 | tf_op jit(solution)/shard_map/all_to_all | solution.py:510
  11.7 1.3 %collective-permute-start.1 = (bf16[16,8,256]{2,1,0:T(8,128)(2,1)}, bf16[16,8,256]{2,1,0:T(8,128)(2,1)S(1)}, u32[]{:S(2)}, u32[]{:S(2)}) collective-permute-start(bf16[16,8,256]{2,1,0:T(8,128)(2,1)} %charges.1), channel_id=1, source_target_pairs={{1,0},{2,1},{3,2},{4,3},{5,4},{6,5},{7,6},{8,7},{9,8},{10,9},{11,1... | collective-permute-start | bytes 196616 | tf_op jit(solution)/shard_map/ppermute | solution.py:436
  13.0 0.0 copy-start.4
  13.0 0.8 %copy-done.4 = bf16[16,8,256]{2,1,0:T(8,128)(2,1)S(1)} copy-done((bf16[16,8,256]{2,1,0:T(8,128)(2,1)S(1)}, bf16[16,8,256]{2,1,0:T(8,128)(2,1)}, u32[]{:S(2)}) %copy-start.4) | copy-done | bytes 65560
  13.9 0.0 copy-start.6
  13.9 0.7 %copy-done.6 = f32[8,128]{1,0:T(8,128)S(1)} copy-done((f32[8,128]{1,0:T(8,128)S(1)}, f32[8,128]{1,0:T(8,128)}, u32[]{:S(2)}) %copy-start.6) | copy-done | bytes 4120
  14.6 0.0 copy-start.7
  14.6 0.7 %copy-done.7 = s32[32,2]{0,1:T(2,128)S(1)} copy-done((s32[32,2]{0,1:T(2,128)S(1)}, s32[32,2]{0,1:T(2,128)}, u32[]{:S(2)}) %copy-start.7) | copy-done | bytes 280
  15.2 5.0 %near.1 = (f32[16,8,256]{2,1,0:T(8,128)S(1)}, bf16[16,8,256]{2,1,0:T(8,128)(2,1)S(1)}) custom-call(s32[2,32]{1,0:T(2,128)S(1)} %bitcast.15, f32[8,128]{1,0:T(8,128)S(1)} %copy-done.6, bf16[16,8,256]{2,1,0:T(8,128)(2,1)S(1)} %copy-done.4, bf16[16,256,256]{2,1,0:T(8,128)(2,1)} %self_blocks.1, bf16[32,256,256]{2,1,0:T(8,128)(2,1)} %near_blocks.3), custom_call_target="tpu_custom_call" | custom-call | flops 80000000 | bytes 20000000 | tf_op jit(solution)/shard_map/near/pallas_call | solution.py:515
  20.2 0.0 copy-start
  20.3 0.0 copy-start.1
  20.3 0.0 copy-start.5
  20.3 0.0 copy-start.8
  20.3 0.0 copy-start.9
  20.3 0.0 copy-start.2
  20.3 0.0 copy-start.3
  20.3 3.2 %collective-permute-start = (bf16[16,8,256]{2,1,0:T(8,128)(2,1)S(1)}, bf16[16,8,256]{2,1,0:T(8,128)(2,1)S(1)}, u32[]{:S(2)}, u32[]{:S(2)}) collective-permute-start(bf16[16,8,256]{2,1,0:T(8,128)(2,1)S(1)} %get-tuple-element.17), channel_id=1, source_target_pairs={{0,1},{1,2},{2,3},{3,4},{4,5},{5,6},{6,7},{7,8},{8,9},{9,10},{10,1... | collective-permute-start | bytes 196616 | tf_op jit(solution)/shard_map/ppermute | solution.py:436
  23.5 0.0 collective-permute-done.1.following
  23.5 3.7 %cross.1.refs_2_.near_own = f32[16,8,256]{2,1,0:T(8,128)S(1)} custom-call(s32[2,32]{1,0:T(2,128)S(1)} %bitcast.16, f32[16,8,256]{2,1,0:T(8,128)S(1)} %get-tuple-element.18.near_own, bf16[16,8,256]{2,1,0:T(8,128)(2,1)S(1)} %collective-permute-done.1.following, bf16[32,256,256]{2,1,0:T(8,128)(2,1)} %near_blocks.3), custom_call_target="tpu_custom_call" | custom-call | flops 32000000 | bytes 8000000 | tf_op jit(solution)/shard_map/cross/pallas_call | solution.py:535
  27.3 0.0 collective-permute-done.refs_1_.near_back
  27.3 0.0 all-to-all-done
  27.3 1.7 %collective-permute-start.2 = (bf16[128,768]{1,0:T(8,128)(2,1)S(1)}, bf16[128,768]{1,0:T(8,128)(2,1)S(1)}, u32[]{:S(2)}, u32[]{:S(2)}) collective-permute-start(bf16[128,768]{1,0:T(8,128)(2,1)S(1)} %slice.4), channel_id=1, source_target_pairs={{0,1},{1,0},{2,3},{3,2},{4,5},{5,4},{6,7},{7,6},{8,9},{9,8},{10,11... | collective-permute-start | bytes 589832 | tf_op jit(solution)/shard_map/ppermute | solution.py:553
  29.0 0.0 copy-done
  29.0 0.0 copy-done.1
  29.0 0.0 copy-done.5
  29.0 0.0 copy-done.8
  29.0 0.0 copy-done.9
  29.0 1.2 %far.1 = (f32[16,256]{1,0:T(8,128)S(1)}, f32[16,512]{1,0:T(8,128)S(1)}, bf16[32,64,64]{2,1,0:T(8,128)(2,1)S(1)}, bf16[32,128]{1,0:T(8,128)(2,1)S(1)}, bf16[64,25...) custom-call(bf16[128,1920]{1,0:T(8,128)(2,1)S(1)} %after.1.got, s32[2,128]{1,0:T(2,128)S(1)} %bitcast.12, ...), custom_call_target="tpu_custom_call" | custom-call | flops 32000000 | bytes 8000000 | tf_op jit(solution)/shard_map/far/pallas_call | solution.py:557
  30.3 0.0 collective-permute-done.2.mom2
  30.3 0.0 copy-done.2
  30.3 0.0 copy-done.3
  30.3 2.9 %downward.1 = f32[16,8,256]{2,1,0:T(8,128)} custom-call(s32[2,128]{1,0:T(2,128)S(1)} %bitcast.13, f32[16,256]{1,0:T(8,128)S(1)} %get-tuple-element.19.half, f32[16,512]{1,0:T(8,128)S(1)} %get-tuple-element.20.back, bf16[128,768]{1,0:T(8,128)(2,1)S(1)} %collective-permute-done.2.mom2, bf16[128,1920]{1,0:T(8,128)(2,1)S(1)} %after.1.got, ...), custom_call_target="tpu_custom_call" | custom-call | tf_op jit(solution)/shard_map/downward/pallas_call | solution.py:575
  (2 shorter events, 0.0 us)
Async XLA Ops:
  4.3 22.9 %all-to-all-start = ((bf16[16,8,1920]{2,1,0:T(8,128)(2,1)}), bf16[16,8,1920]{2,1,0:T(8,128)(2,1)S(1)}, u32[]{:S(2)}, u32[]{:S(2)}) async-start(bf16[16,8,1920]{2,1,0:T(8,128)(2,1)} %bitcast.21), calls=%async_computation | async-start | bytes 983040 | tf_op jit(solution)/shard_map/all_to_all | solution.py:510
  11.7 11.8 %collective-permute-start.1 = (bf16[16,8,256]{2,1,0:T(8,128)(2,1)}, bf16[16,8,256]{2,1,0:T(8,128)(2,1)S(1)}, u32[]{:S(2)}, u32[]{:S(2)}) collective-permute-start(bf16[16,8,256]{2,1,0:T(8,128)(2,1)} %charges.1), channel_id=1, source_target_pairs={{1,0},{2,1},{3,2},{4,3},{5,4},{6,5},{7,6},{8,7},{9,8},{10,9},{11,1... | collective-permute-start | bytes 196616 | tf_op jit(solution)/shard_map/ppermute | solution.py:436
  13.0 0.8 %copy-start.4 = (bf16[16,8,256]{2,1,0:T(8,128)(2,1)S(1)}, bf16[16,8,256]{2,1,0:T(8,128)(2,1)}, u32[]{:S(2)}) copy-start(bf16[16,8,256]{2,1,0:T(8,128)(2,1)} %charges.1) | copy-start | bytes 196612
  13.9 0.7 %copy-start.6 = (f32[8,128]{1,0:T(8,128)S(1)}, f32[8,128]{1,0:T(8,128)}, u32[]{:S(2)}) copy-start(f32[8,128]{1,0:T(8,128)} %get-tuple-element.16.earlier) | copy-start | bytes 12292
  14.6 0.7 %copy-start.7 = (s32[32,2]{0,1:T(2,128)S(1)}, s32[32,2]{0,1:T(2,128)}, u32[]{:S(2)}) copy-start(s32[32,2]{0,1:T(2,128)} %param.14) | copy-start | bytes 772
  20.2 8.8 %copy-start = (bf16[128,64,64]{0,2,1:T(8,128)(2,1)S(1)}, bf16[128,64,64]{0,2,1:T(8,128)(2,1)}, u32[]{:S(2)}) copy-start(bf16[128,64,64]{0,2,1:T(8,128)(2,1)} %param.19) | copy-start | bytes 3145732
  20.3 8.8 %copy-start.1 = (bf16[32,64,64]{2,1,0:T(8,128)(2,1)S(1)}, bf16[32,64,64]{2,1,0:T(8,128)(2,1)}, u32[]{:S(2)}) copy-start(bf16[32,64,64]{2,1,0:T(8,128)(2,1)} %par_c.1) | copy-start | bytes 786436
  20.3 8.8 %copy-start.5 = (s32[128,2]{0,1:T(2,128)S(1)}, s32[128,2]{0,1:T(2,128)}, u32[]{:S(2)}) copy-start(s32[128,2]{0,1:T(2,128)} %param.18) | copy-start | bytes 3076
  20.3 8.8 %copy-start.8 = (s32[32,2]{0,1:T(2,128)S(1)}, s32[32,2]{0,1:T(2,128)}, u32[]{:S(2)}) copy-start(s32[32,2]{0,1:T(2,128)} %param.20) | copy-start | bytes 772
  20.3 8.7 %copy-start.9 = (s32[16]{0:T(128)S(1)}, s32[16]{0:T(128)}, u32[]{:S(2)}) copy-start(s32[16]{0:T(128)} %param.17) | copy-start | bytes 196
  20.3 10.0 %copy-start.2 = (bf16[16,64,256]{2,1,0:T(8,128)(2,1)S(1)}, bf16[16,64,256]{2,1,0:T(8,128)(2,1)}, u32[]{:S(2)}) copy-start(bf16[16,64,256]{2,1,0:T(8,128)(2,1)} %bases.1) | copy-start | bytes 1572868
  20.3 10.0 %copy-start.3 = (bf16[16,64,64]{2,1,0:T(8,128)(2,1)S(1)}, bf16[16,64,64]{2,1,0:T(8,128)(2,1)}, u32[]{:S(2)}) copy-start(bf16[16,64,64]{2,1,0:T(8,128)(2,1)} %transfers.1) | copy-start | bytes 393220
  20.3 6.9 %collective-permute-start = (bf16[16,8,256]{2,1,0:T(8,128)(2,1)S(1)}, bf16[16,8,256]{2,1,0:T(8,128)(2,1)S(1)}, u32[]{:S(2)}, u32[]{:S(2)}) collective-permute-start(bf16[16,8,256]{2,1,0:T(8,128)(2,1)S(1)} %get-tuple-element.17), channel_id=1, source_target_pairs={{0,1},{1,2},{2,3},{3,4},{4,5},{5,6},{6,7},{7,8},{8,9},{9,10},{10,1... | collective-permute-start | bytes 196616 | tf_op jit(solution)/shard_map/ppermute | solution.py:436
  27.3 3.0 %collective-permute-start.2 = (bf16[128,768]{1,0:T(8,128)(2,1)S(1)}, bf16[128,768]{1,0:T(8,128)(2,1)S(1)}, u32[]{:S(2)}, u32[]{:S(2)}) collective-permute-start(bf16[128,768]{1,0:T(8,128)(2,1)S(1)} %slice.4), channel_id=1, source_target_pairs={{0,1},{1,0},{2,3},{3,2},{4,5},{5,4},{6,7},{7,6},{8,9},{9,8},{10,11... | collective-permute-start | bytes 589832 | tf_op jit(solution)/shard_map/ppermute | solution.py:553
where the time goes:
time: 33.6 us; the launch traced here: 33.2 us
  Pallas kernels  17.1 us (51%)
  starting transfers between devices  13.6 us (40%)
  local copies, waits for them, and re-layouts  2.26 us (7%)
    all_to_all x1, starting transfers between devices, on_device(): got = lax.all_to_all(send, 'sfc', split_axis=0, concat_axis=0, tiled=True)  7.4 us
    pallas_call x1, Pallas kernels, on_device(): pl.pallas_call(near_kernel, grid=(steps,), out_shape=[jax.ShapeDtypeStruc...  5 us
    ppermute x2, starting transfers between devices, passed_along(): lax.ppermute(value, axis, [(source, source + steps) for source in range(l...  4.46 us
    pallas_call x1, Pallas kernels, on_device(): pl.pallas_call(pre_kernel, out_shape=[jax.ShapeDtypeStruct((rows, columns...  4.31 us
    pallas_call x1, Pallas kernels, on_device(): pl.pallas_call(cross_kernel, grid=(steps,), out_shape=jax.ShapeDtypeStruc...  3.74 us
    pallas_call x1, Pallas kernels, on_device(): pl.pallas_call(post_kernel, out_shape=jax.ShapeDtypeStruct((leaves, rhs,...  2.86 us
    unnamed x20, local copies, waits for them, and re-layouts  2.24 us
    ppermute x1, starting transfers between devices, on_device(): lax.ppermute(got[:, 2 * width + LANES:], 'sfc', [(i, i ^ 1) for i in rang...  1.71 us
  transfers between devices with their start and end apart: 4, of which 0 were waited for; matrix products, arithmetic and copies ran while one was open for 0% of the time, Pallas kernels for 30%

commit v1 on v0

--- a/solution.py
+++ b/solution.py
@@ -528,7 +528,7 @@
         ],
         out_specs=[whole(leaves, rhs, panels)] * 2,
         scratch_shapes=[pltpu.VMEM((2 * leaves, rhs, panels), F32)],
-        compiler_params=near_params,
+        compiler_params=params,
         cost_estimate=cost(20_000_000),
         name="near",
     )(near_pairs, token, charges, self_blocks, near_blocks)

time: 33.6 us -> 34 us (1.012)
  the two profiles are of different devices: /device:TPU:0 before, /device:TPU:13 now
where the time goes in v1:
time: 34 us; the launch traced here: 33.6 us
  Pallas kernels  17.9 us (53%)
  starting transfers between devices  13.2 us (39%)
  waiting for transfers between devices  1.41 us (4%)
  local copies, waits for them, and re-layouts  0.96 us (3%)
    ppermute x2, starting transfers between devices, passed_along(): lax.ppermute(value, axis, [(source, source + steps) for source in range(l...  6.58 us
    all_to_all x1, starting transfers between devices, on_device(): got = lax.all_to_all(send, 'sfc', split_axis=0, concat_axis=0, tiled=True)  6.57 us
    pallas_call x1, Pallas kernels, on_device(): pl.pallas_call(near_kernel, grid=(steps,), out_shape=[jax.ShapeDtypeStruc...  5.74 us
    pallas_call x1, Pallas kernels, on_device(): pl.pallas_call(pre_kernel, out_shape=[jax.ShapeDtypeStruct((rows, columns...  4.32 us
    pallas_call x1, Pallas kernels, on_device(): pl.pallas_call(cross_kernel, grid=(steps,), out_shape=jax.ShapeDtypeStruc...  3.73 us
    pallas_call x1, Pallas kernels, on_device(): pl.pallas_call(post_kernel, out_shape=jax.ShapeDtypeStruct((leaves, rhs,...  2.86 us
    ppermute x2, waiting for transfers between devices, passed_along(): lax.ppermute(value, axis, [(source, source + steps) for source in range(l...  1.24 us
    pallas_call x1, Pallas kernels, on_device(): pl.pallas_call(far_kernel, out_shape=[jax.ShapeDtypeStruct((leaves, width...  1.22 us
  transfers between devices with their start and end apart: 4, of which 2 were waited for; matrix products, arithmetic and copies ran while one was open for 0% of the time, Pallas kernels for 32%

profile of v1, /device:TPU:13, one launch (start us, length us, event | category | flops | bytes accessed | tf_op | source)
XLA Modules:
  0.0 33.6 jit_solution(6814192461624222600)
XLA Ops:
  0.0 4.3 %upward.1 = (bf16[128,1920]{1,0:T(8,128)(2,1)}, f32[8,128]{1,0:T(8,128)}) custom-call(bf16[16,8,256]{2,1,0:T(8,128)(2,1)} %charges.1, bf16[16,64,256]{2,1,0:T(8,128)(2,1)} %bases.1, bf16[16,64,64]{2,1,0:T(8,128)(2,1)} %transfers.1, s32[1,16]{1,0:T(1,128)} %bitcast.19, s32[2,128]{1,0:T(2,128)} %bitcast.11, bf16[64,64,128]{2,1,0:T(8,128)(2,1)} %bitcast.8, ...), custom_call_target="tpu_custom_call" | custom-call | flops 40000000 | bytes 10000000 | tf_op jit(solution)/shard_map/upward/pallas_call | solution.py:480
  4.3 0.0 copy-start.6
  4.3 6.6 %all-to-all-start = ((bf16[16,8,1920]{2,1,0:T(8,128)(2,1)}), bf16[16,8,1920]{2,1,0:T(8,128)(2,1)S(1)}, u32[]{:S(2)}, u32[]{:S(2)}) async-start(bf16[16,8,1920]{2,1,0:T(8,128)(2,1)} %bitcast.21), calls=%async_computation | async-start | bytes 983040 | tf_op jit(solution)/shard_map/all_to_all | solution.py:510
  10.9 2.3 %collective-permute-start.1 = (bf16[16,8,256]{2,1,0:T(8,128)(2,1)}, bf16[16,8,256]{2,1,0:T(8,128)(2,1)S(1)}, u32[]{:S(2)}, u32[]{:S(2)}) collective-permute-start(bf16[16,8,256]{2,1,0:T(8,128)(2,1)} %charges.1), channel_id=1, source_target_pairs={{1,0},{2,1},{3,2},{4,3},{5,4},{6,5},{7,6},{8,7},{9,8},{10,9},{11,1... | collective-permute-start | bytes 196616 | tf_op jit(solution)/shard_map/ppermute | solution.py:436
  13.2 0.0 copy-start.5
  13.2 0.0 copy-start.7
  13.2 0.0 copy-start.8
  13.2 5.7 %near.1 = (f32[16,8,256]{2,1,0:T(8,128)}, bf16[16,8,256]{2,1,0:T(8,128)(2,1)}) custom-call(s32[2,32]{1,0:T(2,128)} %bitcast.15, f32[8,128]{1,0:T(8,128)} %get-tuple-element.16.earlier, bf16[16,8,256]{2,1,0:T(8,128)(2,1)} %charges.1, bf16[16,256,256]{2,1,0:T(8,128)(2,1)} %self_blocks.1, bf16[32,256,256]{2,1,0:T(8,128)(2,1)} %near_blocks.3), custom_call_target="tpu_custom_call" | custom-call | flops 80000000 | bytes 20000000 | tf_op jit(solution)/shard_map/near/pallas_call | solution.py:515
  19.0 0.0 copy-start
  19.0 0.0 copy-start.1
  19.0 0.0 copy-start.2
  19.0 0.0 copy-start.3
  19.0 4.3 %collective-permute-start = (bf16[16,8,256]{2,1,0:T(8,128)(2,1)}, bf16[16,8,256]{2,1,0:T(8,128)(2,1)S(1)}, u32[]{:S(2)}, u32[]{:S(2)}) collective-permute-start(bf16[16,8,256]{2,1,0:T(8,128)(2,1)} %get-tuple-element.17), channel_id=1, source_target_pairs={{0,1},{1,2},{2,3},{3,4},{4,5},{5,6},{6,7},{7,8},{8,9},{9,10},{10,1... | collective-permute-start | bytes 196616 | tf_op jit(solution)/shard_map/ppermute | solution.py:436
  23.3 1.2 %collective-permute-done.1.following = bf16[16,8,256]{2,1,0:T(8,128)(2,1)S(1)} collective-permute-done((bf16[16,8,256]{2,1,0:T(8,128)(2,1)}, bf16[16,8,256]{2,1,0:T(8,128)(2,1)S(1)}, u32[]{:S(2)}, u32[]{:S(2)}) %collective-permute-start.1) | collective-permute-done | bytes 65568 | tf_op jit(solution)/shard_map/ppermute | solution.py:436
  24.5 0.0 copy-done.6
  24.5 0.0 copy-start.4
  24.5 0.9 %copy-done.4 = f32[16,8,256]{2,1,0:T(8,128)S(1)} copy-done((f32[16,8,256]{2,1,0:T(8,128)S(1)}, f32[16,8,256]{2,1,0:T(8,128)}, u32[]{:S(2)}) %copy-start.4) | copy-done | bytes 131096
  25.5 3.7 %cross.1.refs_2_.near_own = f32[16,8,256]{2,1,0:T(8,128)S(1)} custom-call(s32[2,32]{1,0:T(2,128)S(1)} %bitcast.16, f32[16,8,256]{2,1,0:T(8,128)S(1)} %copy-done.4, bf16[16,8,256]{2,1,0:T(8,128)(2,1)S(1)} %collective-permute-done.1.following, bf16[32,256,256]{2,1,0:T(8,128)(2,1)} %near_blocks.3), custom_call_target="tpu_custom_call" | custom-call | flops 32000000 | bytes 8000000 | tf_op jit(solution)/shard_map/cross/pallas_call | solution.py:535
  29.2 0.0 collective-permute-done.refs_1_.near_back
  29.2 0.0 all-to-all-done
  29.2 0.1 collective-permute-start.2
  29.3 0.0 copy-done.5
  29.3 0.0 copy-done.7
  29.3 0.0 copy-done.8
  29.4 0.0 copy-done
  29.4 0.0 copy-done.1
  29.4 1.2 %far.1 = (f32[16,256]{1,0:T(8,128)S(1)}, f32[16,512]{1,0:T(8,128)S(1)}, bf16[32,64,64]{2,1,0:T(8,128)(2,1)S(1)}, bf16[32,128]{1,0:T(8,128)(2,1)S(1)}, bf16[64,25...) custom-call(bf16[128,1920]{1,0:T(8,128)(2,1)S(1)} %after.1.got, s32[2,128]{1,0:T(2,128)S(1)} %bitcast.12, ...), custom_call_target="tpu_custom_call" | custom-call | flops 32000000 | bytes 8000000 | tf_op jit(solution)/shard_map/far/pallas_call | solution.py:557
  30.6 0.2 collective-permute-done.2.mom2
  30.7 0.0 copy-done.2
  30.8 0.0 copy-done.3
  30.8 2.9 %downward.1 = f32[16,8,256]{2,1,0:T(8,128)} custom-call(s32[2,128]{1,0:T(2,128)S(1)} %bitcast.13, f32[16,256]{1,0:T(8,128)S(1)} %get-tuple-element.19.half, f32[16,512]{1,0:T(8,128)S(1)} %get-tuple-element.20.back, bf16[128,768]{1,0:T(8,128)(2,1)S(1)} %collective-permute-done.2.mom2, bf16[128,1920]{1,0:T(8,128)(2,1)S(1)} %after.1.got, ...), custom_call_target="tpu_custom_call" | custom-call | tf_op jit(solution)/shard_map/downward/pallas_call | solution.py:575
  (2 shorter events, 0.0 us)
Async XLA Ops:
  4.3 20.2 %copy-start.6 = (s32[32,2]{0,1:T(2,128)S(1)}, s32[32,2]{0,1:T(2,128)}, u32[]{:S(2)}) copy-start(s32[32,2]{0,1:T(2,128)} %param.14) | copy-start | bytes 772
  4.3 24.9 %all-to-all-start = ((bf16[16,8,1920]{2,1,0:T(8,128)(2,1)}), bf16[16,8,1920]{2,1,0:T(8,128)(2,1)S(1)}, u32[]{:S(2)}, u32[]{:S(2)}) async-start(bf16[16,8,1920]{2,1,0:T(8,128)(2,1)} %bitcast.21), calls=%async_computation | async-start | bytes 983040 | tf_op jit(solution)/shard_map/all_to_all | solution.py:510
  10.9 13.6 %collective-permute-start.1 = (bf16[16,8,256]{2,1,0:T(8,128)(2,1)}, bf16[16,8,256]{2,1,0:T(8,128)(2,1)S(1)}, u32[]{:S(2)}, u32[]{:S(2)}) collective-permute-start(bf16[16,8,256]{2,1,0:T(8,128)(2,1)} %charges.1), channel_id=1, source_target_pairs={{1,0},{2,1},{3,2},{4,3},{5,4},{6,5},{7,6},{8,7},{9,8},{10,9},{11,1... | collective-permute-start | bytes 196616 | tf_op jit(solution)/shard_map/ppermute | solution.py:436
  13.2 16.1 %copy-start.5 = (s32[128,2]{0,1:T(2,128)S(1)}, s32[128,2]{0,1:T(2,128)}, u32[]{:S(2)}) copy-start(s32[128,2]{0,1:T(2,128)} %param.18) | copy-start | bytes 3076
  13.2 16.1 %copy-start.7 = (s32[32,2]{0,1:T(2,128)S(1)}, s32[32,2]{0,1:T(2,128)}, u32[]{:S(2)}) copy-start(s32[32,2]{0,1:T(2,128)} %param.20) | copy-start | bytes 772
  13.2 16.1 %copy-start.8 = (s32[16]{0:T(128)S(1)}, s32[16]{0:T(128)}, u32[]{:S(2)}) copy-start(s32[16]{0:T(128)} %param.17) | copy-start | bytes 196
  19.0 10.4 %copy-start = (bf16[128,64,64]{0,2,1:T(8,128)(2,1)S(1)}, bf16[128,64,64]{0,2,1:T(8,128)(2,1)}, u32[]{:S(2)}) copy-start(bf16[128,64,64]{0,2,1:T(8,128)(2,1)} %param.19) | copy-start | bytes 3145732
  19.0 10.4 %copy-start.1 = (bf16[32,64,64]{2,1,0:T(8,128)(2,1)S(1)}, bf16[32,64,64]{2,1,0:T(8,128)(2,1)}, u32[]{:S(2)}) copy-start(bf16[32,64,64]{2,1,0:T(8,128)(2,1)} %par_c.1) | copy-start | bytes 786436
  19.0 11.8 %copy-start.2 = (bf16[16,64,256]{2,1,0:T(8,128)(2,1)S(1)}, bf16[16,64,256]{2,1,0:T(8,128)(2,1)}, u32[]{:S(2)}) copy-start(bf16[16,64,256]{2,1,0:T(8,128)(2,1)} %bases.1) | copy-start | bytes 1572868
  19.0 11.8 %copy-start.3 = (bf16[16,64,64]{2,1,0:T(8,128)(2,1)S(1)}, bf16[16,64,64]{2,1,0:T(8,128)(2,1)}, u32[]{:S(2)}) copy-start(bf16[16,64,64]{2,1,0:T(8,128)(2,1)} %transfers.1) | copy-start | bytes 393220
  19.0 10.2 %collective-permute-start = (bf16[16,8,256]{2,1,0:T(8,128)(2,1)}, bf16[16,8,256]{2,1,0:T(8,128)(2,1)S(1)}, u32[]{:S(2)}, u32[]{:S(2)}) collective-permute-start(bf16[16,8,256]{2,1,0:T(8,128)(2,1)} %get-tuple-element.17), channel_id=1, source_target_pairs={{0,1},{1,2},{2,3},{3,4},{4,5},{5,6},{6,7},{7,8},{8,9},{9,10},{10,1... | collective-permute-start | bytes 196616 | tf_op jit(solution)/shard_map/ppermute | solution.py:436
  24.5 0.9 %copy-start.4 = (f32[16,8,256]{2,1,0:T(8,128)S(1)}, f32[16,8,256]{2,1,0:T(8,128)}, u32[]{:S(2)}) copy-start(f32[16,8,256]{2,1,0:T(8,128)} %get-tuple-element.18.near_own) | copy-start | bytes 393220
  29.2 1.5 %collective-permute-start.2 = (bf16[128,768]{1,0:T(8,128)(2,1)S(1)}, bf16[128,768]{1,0:T(8,128)(2,1)S(1)}, u32[]{:S(2)}, u32[]{:S(2)}) collective-permute-start(bf16[128,768]{1,0:T(8,128)(2,1)S(1)} %slice.4), channel_id=1, source_target_pairs={{0,1},{1,0},{2,3},{3,2},{4,5},{5,4},{6,7},{7,6},{8,9},{9,8},{10,11... | collective-permute-start | bytes 589832 | tf_op jit(solution)/shard_map/ppermute | solution.py:553
